TPU v7x, 256 devices: a whole 4x4x8 slice. The times are simulated.
256 devices in a mesh: lat: 32 (over y_lo, z, core), lon: 8 (over y_hi, x).
Axes of the slice: x: 4, y: 4 (y_hi: 2, y_lo: 2; y = y_hi * 2 + y_lo), z: 8, core: 2. Of those that a mesh axis runs over, the one named last changes fastest.
Arguments:
- cotangent: bfloat16 [384, 384, 1024], P(None, 'lat', 'lon'), may hold values from -6 to 6
- layer_input: bfloat16 [384, 384, 1024], P(None, 'lat', 'lon'), may hold values from -6 to 6
- filter_values: bfloat16 [3, 384, 4, 17], replicated, may hold values from -4 to 4
- weights: bfloat16 [3, 384, 384], replicated, may hold values from -0.1875 to 0.1875
- row_offset: int32 [384], replicated, may hold values from -3 to 0, as said below
- reach: int32 [384], replicated, may hold values from 1 to 9, as said below
Outputs:
- input_grad: bfloat16 [384, 384, 1024], P(None, 'lat', 'lon')
- weight_grad: float32 [3, 384, 384], replicated
Inputs may be any that keep to these rules, and one draw needn't show every extreme that they name: The support rows of output latitude o are o + row_offset[o] to o + row_offset[o] + 3. Taps d with |d| < reach[o] are used.
All inputs are finite; a program needn't handle non-finite values.
Results may differ from a plain program's by a relative error of at most 0.0049.
Values may be sent and summed in bfloat16 or wider, within the bound.
A program may use at most 128 MiB of HBM per device.

v0:
```python
import jax
import jax.numpy as jnp
from jax import lax
from jax.sharding import PartitionSpec as P


def with_halo(x, sides, width):
    for axis, dim in sides:
        devices, length = (lax.axis_size(axis), x.shape[dim])
        up = [(i, (i + 1) % devices) for i in range(devices - 1)]
        down = [(j, i) for i, j in up]
        last = lax.slice_in_dim(x, length - width, length, axis=dim)
        first = lax.slice_in_dim(x, 0, width, axis=dim)
        before = lax.ppermute(last, axis, up)
        after = lax.ppermute(first, axis, down)
        x = jnp.concatenate([before, x, after], axis=dim)
    return x


def on_device(cotangent, layer_input, filter_values, weights, row_offset, reach):
    feature_channels, rows, cols = cotangent.shape
    kernels, nlat, span, taps = filter_values.shape
    reach_q = (taps - 1) // 2
    rim = span - 1
    tall = rows + 2 * rim
    first_row = lax.axis_index("lat") * rows
    padded = with_halo(cotangent, (("lat", 1),), rim)
    source = first_row - rim + jnp.arange(tall, dtype=jnp.int32)
    inside = (source >= 0) & (source < nlat)
    safe = jnp.clip(source, 0, nlat - 1)
    offsets = jnp.take(row_offset, safe)
    tap_reach_list = jnp.where(inside, jnp.take(reach, safe), 0)
    psi_rows = jnp.take(filter_values, safe, axis=1).astype(jnp.float32)
    tap_ids = jnp.arange(taps, dtype=jnp.int32) - reach_q
    live = (jnp.abs(tap_ids)[None, :] < tap_reach_list[:, None]).astype(jnp.float32)
    level = (
        jnp.arange(rows, dtype=jnp.int32)[:, None]
        - jnp.arange(tall, dtype=jnp.int32)[None, :]
        + rim
        - offsets[None, :]
    )
    pick = (level[:, :, None] == jnp.arange(span, dtype=jnp.int32)[None, None, :]).astype(
        jnp.float32
    )
    mixing = jnp.einsum("ios,kost->ktio", pick, psi_rows * live[None, :, None, :]).astype(
        jnp.bfloat16
    )
    widest = jnp.max(tap_reach_list)
    lower = reach_q - widest + 1
    upper = reach_q + widest
    moved = lax.all_to_all(padded, "lon", split_axis=0, concat_axis=2, tiled=True)
    wide = jnp.concatenate([moved[:, :, -reach_q:], moved, moved[:, :, :reach_q]], axis=2)
    out_cols = wide.shape[2] - 2 * reach_q
    local_channels = wide.shape[0]

    def add_tap(tap, total):
        shifted = lax.dynamic_slice_in_dim(wide, 2 * reach_q - tap, out_cols, 2)
        mix_tap = lax.dynamic_index_in_dim(mixing, tap, 1, keepdims=False)
        return total + jnp.einsum(
            "kio,col->kcil", mix_tap, shifted, preferred_element_type=jnp.float32
        )

    start = jnp.zeros((kernels, local_channels, rows, out_cols), jnp.float32)
    tap_spread_width = lax.fori_loop(lower, upper, add_tap, start).astype(jnp.bfloat16)
    tap_spread_width = lax.all_to_all(
        tap_spread_width, "lon", split_axis=3, concat_axis=1, tiled=True
    )
    input_grad = lax.dot_general(
        weights, tap_spread_width, (((0, 1), (0, 1)), ((), ())), preferred_element_type=jnp.float32
    )
    partial_grad = lax.dot_general(
        tap_spread_width,
        layer_input,
        (((2, 3), (1, 2)), ((), ())),
        preferred_element_type=jnp.float32,
    )
    total_grad = lax.psum(partial_grad, ("lat", "lon"))
    longitude_count_full = cols * lax.axis_size("lon")
    weight_grad = total_grad / jnp.sqrt(jnp.float32(nlat * longitude_count_full))
    return (input_grad.astype(jnp.bfloat16), weight_grad)


def solution(mesh):
    return jax.shard_map(
        on_device,
        mesh=mesh,
        in_specs=(P(None, "lat", "lon"), P(None, "lat", "lon"), P(), P(), P(), P()),
        out_specs=(P(None, "lat", "lon"), P()),
        check_vma=False,
    )
```

profile of v0, /device:TPU:2, one launch (start us, length us, event | category | flops | bytes accessed | tf_op | source)
XLA Modules:
  0.0 651.0 jit_solution(12407384555351623323)
XLA Ops:
  40.9 13.7 %all-to-all-done = bf16[384,18,128]{2,1,0:T(8,128)(2,1)S(1)} async-done(((bf16[384,18,128]{2,1,0:T(8,128)(2,1)}), bf16[384,18,128]{2,1,0:T(8,128)(2,1)S(1)}, u32[]{:S(2)}, u32[]{:S(2)}) %all-to-all-start) | async-done | bytes 1769504 | tf_op jit(solution)/shard_map/all_to_all | solution.py:51
  70.2 183.5 %while.12 = (s32[]{:T(128)}, f32[3,48,12,1024]{3,2,0,1:T(8,128)}, s32[]{:T(128)}, bf16[48,18,1040]{2,0,1:T(8,128)(2,1)S(1)}, bf16[3,17,12,18]{3,2,0,1:T(8,128)(2...) while((s32[]{:T(128)}, f32[3,48,12,1024]{3,2,0,1:T(8,128)}, s32[]{:T(128)}, ...), condition=%wide.region_2.4_spmd, body=%wide.region_1.3_spmd.sunk | while | flops 65470472 | bytes 21835972 | solution.py:64
  71.0 10.0 %bitcast_add_fusion.2 = f32[3,48,12,1024]{3,2,0,1:T(8,128)} fusion(f32[3,48,12,1024]{3,2,0,1:T(8,128)} %get-tuple-element.167, bf16[48,18,1024]{2,0,1:T(8,128)(2,1)S(1)} %constant_dynamic-slice_fusion.2, bf16[3,17,12,18]{3,2,0,1:T(8,128)(2,1)} %get-tuple-element.180, s32[]{:T(128)S(6)} %select_n.77), kind=kOutput, calls=%fused_computation.3.clone.1 | convolution fusion | flops 65470464 | bytes 18296836 | tf_op jit(solution)/shard_map/while/body/kio,col->kcil/dot_general | solution.py:59
  81.8 10.0 %bitcast_add_fusion.2 = f32[3,48,12,1024]{3,2,0,1:T(8,128)} fusion(f32[3,48,12,1024]{3,2,0,1:T(8,128)} %get-tuple-element.167, bf16[48,18,1024]{2,0,1:T(8,128)(2,1)S(1)} %constant_dynamic-slice_fusion.2, bf16[3,17,12,18]{3,2,0,1:T(8,128)(2,1)} %get-tuple-element.180, s32[]{:T(128)S(6)} %select_n.77), kind=kOutput, calls=%fused_computation.3.clone.1 | convolution fusion | flops 65470464 | bytes 18296836 | tf_op jit(solution)/shard_map/while/body/kio,col->kcil/dot_general | solution.py:59
  92.6 10.0 %bitcast_add_fusion.2 = f32[3,48,12,1024]{3,2,0,1:T(8,128)} fusion(f32[3,48,12,1024]{3,2,0,1:T(8,128)} %get-tuple-element.167, bf16[48,18,1024]{2,0,1:T(8,128)(2,1)S(1)} %constant_dynamic-slice_fusion.2, bf16[3,17,12,18]{3,2,0,1:T(8,128)(2,1)} %get-tuple-element.180, s32[]{:T(128)S(6)} %select_n.77), kind=kOutput, calls=%fused_computation.3.clone.1 | convolution fusion | flops 65470464 | bytes 18296836 | tf_op jit(solution)/shard_map/while/body/kio,col->kcil/dot_general | solution.py:59
  103.4 10.0 %bitcast_add_fusion.2 = f32[3,48,12,1024]{3,2,0,1:T(8,128)} fusion(f32[3,48,12,1024]{3,2,0,1:T(8,128)} %get-tuple-element.167, bf16[48,18,1024]{2,0,1:T(8,128)(2,1)S(1)} %constant_dynamic-slice_fusion.2, bf16[3,17,12,18]{3,2,0,1:T(8,128)(2,1)} %get-tuple-element.180, s32[]{:T(128)S(6)} %select_n.77), kind=kOutput, calls=%fused_computation.3.clone.1 | convolution fusion | flops 65470464 | bytes 18296836 | tf_op jit(solution)/shard_map/while/body/kio,col->kcil/dot_general | solution.py:59
  114.2 10.0 %bitcast_add_fusion.2 = f32[3,48,12,1024]{3,2,0,1:T(8,128)} fusion(f32[3,48,12,1024]{3,2,0,1:T(8,128)} %get-tuple-element.167, bf16[48,18,1024]{2,0,1:T(8,128)(2,1)S(1)} %constant_dynamic-slice_fusion.2, bf16[3,17,12,18]{3,2,0,1:T(8,128)(2,1)} %get-tuple-element.180, s32[]{:T(128)S(6)} %select_n.77), kind=kOutput, calls=%fused_computation.3.clone.1 | convolution fusion | flops 65470464 | bytes 18296836 | tf_op jit(solution)/shard_map/while/body/kio,col->kcil/dot_general | solution.py:59
  125.0 10.0 %bitcast_add_fusion.2 = f32[3,48,12,1024]{3,2,0,1:T(8,128)} fusion(f32[3,48,12,1024]{3,2,0,1:T(8,128)} %get-tuple-element.167, bf16[48,18,1024]{2,0,1:T(8,128)(2,1)S(1)} %constant_dynamic-slice_fusion.2, bf16[3,17,12,18]{3,2,0,1:T(8,128)(2,1)} %get-tuple-element.180, s32[]{:T(128)S(6)} %select_n.77), kind=kOutput, calls=%fused_computation.3.clone.1 | convolution fusion | flops 65470464 | bytes 18296836 | tf_op jit(solution)/shard_map/while/body/kio,col->kcil/dot_general | solution.py:59
  135.8 10.0 %bitcast_add_fusion.2 = f32[3,48,12,1024]{3,2,0,1:T(8,128)} fusion(f32[3,48,12,1024]{3,2,0,1:T(8,128)} %get-tuple-element.167, bf16[48,18,1024]{2,0,1:T(8,128)(2,1)S(1)} %constant_dynamic-slice_fusion.2, bf16[3,17,12,18]{3,2,0,1:T(8,128)(2,1)} %get-tuple-element.180, s32[]{:T(128)S(6)} %select_n.77), kind=kOutput, calls=%fused_computation.3.clone.1 | convolution fusion | flops 65470464 | bytes 18296836 | tf_op jit(solution)/shard_map/while/body/kio,col->kcil/dot_general | solution.py:59
  146.6 10.0 %bitcast_add_fusion.2 = f32[3,48,12,1024]{3,2,0,1:T(8,128)} fusion(f32[3,48,12,1024]{3,2,0,1:T(8,128)} %get-tuple-element.167, bf16[48,18,1024]{2,0,1:T(8,128)(2,1)S(1)} %constant_dynamic-slice_fusion.2, bf16[3,17,12,18]{3,2,0,1:T(8,128)(2,1)} %get-tuple-element.180, s32[]{:T(128)S(6)} %select_n.77), kind=kOutput, calls=%fused_computation.3.clone.1 | convolution fusion | flops 65470464 | bytes 18296836 | tf_op jit(solution)/shard_map/while/body/kio,col->kcil/dot_general | solution.py:59
  157.4 10.0 %bitcast_add_fusion.2 = f32[3,48,12,1024]{3,2,0,1:T(8,128)} fusion(f32[3,48,12,1024]{3,2,0,1:T(8,128)} %get-tuple-element.167, bf16[48,18,1024]{2,0,1:T(8,128)(2,1)S(1)} %constant_dynamic-slice_fusion.2, bf16[3,17,12,18]{3,2,0,1:T(8,128)(2,1)} %get-tuple-element.180, s32[]{:T(128)S(6)} %select_n.77), kind=kOutput, calls=%fused_computation.3.clone.1 | convolution fusion | flops 65470464 | bytes 18296836 | tf_op jit(solution)/shard_map/while/body/kio,col->kcil/dot_general | solution.py:59
  168.1 10.0 %bitcast_add_fusion.2 = f32[3,48,12,1024]{3,2,0,1:T(8,128)} fusion(f32[3,48,12,1024]{3,2,0,1:T(8,128)} %get-tuple-element.167, bf16[48,18,1024]{2,0,1:T(8,128)(2,1)S(1)} %constant_dynamic-slice_fusion.2, bf16[3,17,12,18]{3,2,0,1:T(8,128)(2,1)} %get-tuple-element.180, s32[]{:T(128)S(6)} %select_n.77), kind=kOutput, calls=%fused_computation.3.clone.1 | convolution fusion | flops 65470464 | bytes 18296836 | tf_op jit(solution)/shard_map/while/body/kio,col->kcil/dot_general | solution.py:59
  178.9 10.0 %bitcast_add_fusion.2 = f32[3,48,12,1024]{3,2,0,1:T(8,128)} fusion(f32[3,48,12,1024]{3,2,0,1:T(8,128)} %get-tuple-element.167, bf16[48,18,1024]{2,0,1:T(8,128)(2,1)S(1)} %constant_dynamic-slice_fusion.2, bf16[3,17,12,18]{3,2,0,1:T(8,128)(2,1)} %get-tuple-element.180, s32[]{:T(128)S(6)} %select_n.77), kind=kOutput, calls=%fused_computation.3.clone.1 | convolution fusion | flops 65470464 | bytes 18296836 | tf_op jit(solution)/shard_map/while/body/kio,col->kcil/dot_general | solution.py:59
  189.7 10.0 %bitcast_add_fusion.2 = f32[3,48,12,1024]{3,2,0,1:T(8,128)} fusion(f32[3,48,12,1024]{3,2,0,1:T(8,128)} %get-tuple-element.167, bf16[48,18,1024]{2,0,1:T(8,128)(2,1)S(1)} %constant_dynamic-slice_fusion.2, bf16[3,17,12,18]{3,2,0,1:T(8,128)(2,1)} %get-tuple-element.180, s32[]{:T(128)S(6)} %select_n.77), kind=kOutput, calls=%fused_computation.3.clone.1 | convolution fusion | flops 65470464 | bytes 18296836 | tf_op jit(solution)/shard_map/while/body/kio,col->kcil/dot_general | solution.py:59
  200.5 10.0 %bitcast_add_fusion.2 = f32[3,48,12,1024]{3,2,0,1:T(8,128)} fusion(f32[3,48,12,1024]{3,2,0,1:T(8,128)} %get-tuple-element.167, bf16[48,18,1024]{2,0,1:T(8,128)(2,1)S(1)} %constant_dynamic-slice_fusion.2, bf16[3,17,12,18]{3,2,0,1:T(8,128)(2,1)} %get-tuple-element.180, s32[]{:T(128)S(6)} %select_n.77), kind=kOutput, calls=%fused_computation.3.clone.1 | convolution fusion | flops 65470464 | bytes 18296836 | tf_op jit(solution)/shard_map/while/body/kio,col->kcil/dot_general | solution.py:59
  211.3 10.0 %bitcast_add_fusion.2 = f32[3,48,12,1024]{3,2,0,1:T(8,128)} fusion(f32[3,48,12,1024]{3,2,0,1:T(8,128)} %get-tuple-element.167, bf16[48,18,1024]{2,0,1:T(8,128)(2,1)S(1)} %constant_dynamic-slice_fusion.2, bf16[3,17,12,18]{3,2,0,1:T(8,128)(2,1)} %get-tuple-element.180, s32[]{:T(128)S(6)} %select_n.77), kind=kOutput, calls=%fused_computation.3.clone.1 | convolution fusion | flops 65470464 | bytes 18296836 | tf_op jit(solution)/shard_map/while/body/kio,col->kcil/dot_general | solution.py:59
  222.1 10.0 %bitcast_add_fusion.2 = f32[3,48,12,1024]{3,2,0,1:T(8,128)} fusion(f32[3,48,12,1024]{3,2,0,1:T(8,128)} %get-tuple-element.167, bf16[48,18,1024]{2,0,1:T(8,128)(2,1)S(1)} %constant_dynamic-slice_fusion.2, bf16[3,17,12,18]{3,2,0,1:T(8,128)(2,1)} %get-tuple-element.180, s32[]{:T(128)S(6)} %select_n.77), kind=kOutput, calls=%fused_computation.3.clone.1 | convolution fusion | flops 65470464 | bytes 18296836 | tf_op jit(solution)/shard_map/while/body/kio,col->kcil/dot_general | solution.py:59
  232.9 10.0 %bitcast_add_fusion.2 = f32[3,48,12,1024]{3,2,0,1:T(8,128)} fusion(f32[3,48,12,1024]{3,2,0,1:T(8,128)} %get-tuple-element.167, bf16[48,18,1024]{2,0,1:T(8,128)(2,1)S(1)} %constant_dynamic-slice_fusion.2, bf16[3,17,12,18]{3,2,0,1:T(8,128)(2,1)} %get-tuple-element.180, s32[]{:T(128)S(6)} %select_n.77), kind=kOutput, calls=%fused_computation.3.clone.1 | convolution fusion | flops 65470464 | bytes 18296836 | tf_op jit(solution)/shard_map/while/body/kio,col->kcil/dot_general | solution.py:59
  262.9 14.4 %copy.54 = bf16[3,48,12,1024]{1,2,0,3:T(8,128)(2,1)} copy(bf16[3,48,12,1024]{3,1,2,0:T(8,128)(2,1)} %copy.71) | data formatting | bytes 7077888 | tf_op jit(solution)/shard_map/convert_element_type | solution.py:64
  277.3 16.4 %reshape.127 = bf16[8,2,110592]{2,1,0:T(2,128)(2,1)} reshape(bf16[1024,3,12,48]{3,2,1,0:T(8,128)(2,1)} %bitcast.63) | data formatting | bytes 7077888
  293.8 52.3 %all_to_all.36 = bf16[8,2,110592]{2,1,0:T(2,128)(2,1)} all-to-all(bf16[8,2,110592]{2,1,0:T(2,128)(2,1)} %reshape.127), channel_id=1, replica_groups=mesh['lat'=32,'lon'=8] {'lon'}, dimensions={0} | all-to-all | bytes 7077888 | tf_op jit(solution)/shard_map/all_to_all | solution.py:65
  346.1 17.7 %reshape.128 = bf16[1024,3,12,48]{3,2,1,0:T(8,128)(2,1)} reshape(bf16[8,2,110592]{2,1,0:T(2,128)(2,1)} %all_to_all.36) | data formatting | bytes 7077888
  363.8 13.7 %copy.56 = bf16[3,8,48,12,128]{4,2,1,3,0:T(8,128)(2,1)} copy(bf16[3,8,48,12,128]{2,3,0,4,1:T(8,128)(2,1)} %bitcast.64) | data formatting | bytes 7077888 | tf_op jit(solution)/shard_map/all_to_all | solution.py:65
  388.5 252.8 %all-reduce.2.cloned.1.call-done = f32[3,384,384]{2,1,0:T(8,128)} async-done(((f32[3,384,384]{2,1,0:T(8,128)}), f32[3,384,384]{2,1,0:T(8,128)}) %all-reduce.2.cloned.1.call-update) | async-done | bytes 1769488 | tf_op jit(solution)/shard_map/psum | solution.py:77
  (65 shorter events, 94.5 us)
Async XLA Ops:
  7.2 370.4 %copy-start = (bf16[384,12,128]{2,0,1:T(8,128)(2,1)S(1)}, bf16[384,12,128]{2,0,1:T(8,128)(2,1)}, u32[]{:S(2)}) copy-start(bf16[384,12,128]{2,0,1:T(8,128)(2,1)} %param.11) | copy-start | bytes 3538948
  9.1 5.8 collective-permute-start
  11.5 4.6 collective-permute-start.1
  19.3 7.6 %copy-start.1 = (s32[384]{0:T(512)S(1)}, s32[384]{0:T(512)}, u32[]{:S(2)}) copy-start(s32[384]{0:T(512)} %param.14) | copy-start | bytes 4612
  19.3 8.3 %copy-start.2 = (s32[384]{0:T(512)S(1)}, s32[384]{0:T(512)}, u32[]{:S(2)}) copy-start(s32[384]{0:T(512)} %param.15) | copy-start | bytes 4612
  19.3 35.4 %all-to-all-start = ((bf16[384,18,128]{2,1,0:T(8,128)(2,1)}), bf16[384,18,128]{2,1,0:T(8,128)(2,1)S(1)}, u32[]{:S(2)}, u32[]{:S(2)}) async-start(bf16[384,18,128]{2,1,0:T(8,128)(2,1)} %pad_maximum_fusion), calls=%async_computation | async-start | bytes 4718592 | tf_op jit(solution)/shard_map/all_to_all | solution.py:51
  26.9 614.5 %all-reduce.2.cloned.1.call-start = ((), (), s32[]{:S(2)}) async-start(), calls=%async_computation.2 | async-start | bytes 3538944 | tf_op jit(solution)/shard_map/psum | solution.py:77
  59.7 1.3 copy-start.3
  377.5 5.3 copy-start.4
Sparse Core Ops, SparseCore 0:
  383.0 258.2 all-reduce.1
where the time goes:
time: 653 us; the launch traced here: 651 us
  waiting for transfers between devices  267 us (41%)
  matrix products  181 us (28%)
  local copies, waits for them, and re-layouts  117 us (18%)
  blocking collectives  52.3 us (8%)
  between operations  15.5 us (2%)
  starting transfers between devices  11.3 us (2%)
  other arithmetic  7.17 us (1%)
    psum x1, waiting for transfers between devices, on_device(): total_grad = lax.psum(partial_grad, ('lat', 'lon'))  253 us
    dot_general x17, matrix products, add_tap(): jnp.einsum('kio,col->kcil', mix_tap, shifted, preferred_element_type=jnp....  170 us
    all_to_all x1, blocking collectives, on_device(): lax.all_to_all(tap_spread_width, 'lon', split_axis=3, concat_axis=1, tile...  52.3 us
    unnamed x15, local copies, waits for them, and re-layouts  41 us
    convert_element_type x1, local copies, waits for them, and re-layouts, on_device(): lax.fori_loop(lower, upper, add_tap, start).astype(jnp.bfloat16)  14.4 us
    all_to_all x1, waiting for transfers between devices, on_device(): lax.all_to_all(padded, 'lon', split_axis=0, concat_axis=2, tiled=True)  13.7 us
    all_to_all x1, local copies, waits for them, and re-layouts, on_device(): lax.all_to_all(tap_spread_width, 'lon', split_axis=3, concat_axis=1, tile...  13.7 us
    dynamic_slice x17, local copies, waits for them, and re-layouts, add_tap(): shifted = lax.dynamic_slice_in_dim(wide, 2 * reach_q - tap, out_cols, 2)  13.6 us
  transfers between devices with their start and end apart: 4, of which 2 were waited for; matrix products, arithmetic and copies ran while one was open for 3% of the time, Pallas kernels for 0%

commit v1 on v0

--- a/solution.py
+++ b/solution.py
@@ -2,6 +2,12 @@
 import jax.numpy as jnp
 from jax import lax
 from jax.sharding import PartitionSpec as P
+
+
+def stacked_exchange(x, axis, split, join):
+    pieces = jnp.split(x, lax.axis_size(axis), axis=split)
+    arrived = lax.all_to_all(jnp.stack(pieces), axis, 0, 0)
+    return jnp.concatenate(arrived, axis=join)
 
 
 def with_halo(x, sides, width):
@@ -62,9 +68,7 @@
 
     start = jnp.zeros((kernels, local_channels, rows, out_cols), jnp.float32)
     tap_spread_width = lax.fori_loop(lower, upper, add_tap, start).astype(jnp.bfloat16)
-    tap_spread_width = lax.all_to_all(
-        tap_spread_width, "lon", split_axis=3, concat_axis=1, tiled=True
-    )
+    tap_spread_width = stacked_exchange(tap_spread_width, "lon", 3, 1)
     input_grad = lax.dot_general(
         weights, tap_spread_width, (((0, 1), (0, 1)), ((), ())), preferred_element_type=jnp.float32
     )

time: 653 us -> 588 us (0.900)
  local copies, waits for them, and re-layouts: 117 us -> 56.8 us
    unnamed x15 -> x22, local copies, waits for them, and re-layouts: 41 us -> 9.46 us
    convert_element_type x1 -> x0, local copies, waits for them, and re-layouts: 14.4 us -> none  [on_device(): lax.fori_loop(lower, upper, add_tap, start).astype(jnp.bfloat16)]
    all_to_all x1, local copies, waits for them, and re-layouts: 13.7 us -> 0.99 us  [stacked_exchange(): arrived = lax.all_to_all(jnp.stack(pieces), axis, 0, 0)]
  transfers between devices with their start and end apart: 4 -> 4, of which waited for: 2 -> 2; matrix products, arithmetic and copies ran while one was open for 3% -> 4% of each run, Pallas kernels for 0% -> 0%
where the time goes in v1:
time: 588 us; the launch traced here: 587 us
  waiting for transfers between devices  266 us (45%)
  matrix products  179 us (30%)
  local copies, waits for them, and re-layouts  56.8 us (10%)
  blocking collectives  50.3 us (9%)
  between operations  15.5 us (3%)
  starting transfers between devices  11.3 us (2%)
  other arithmetic  7.17 us (1%)
    psum x1, waiting for transfers between devices, on_device(): total_grad = lax.psum(partial_grad, ('lat', 'lon'))  253 us
    dot_general x17, matrix products, add_tap(): jnp.einsum('kio,col->kcil', mix_tap, shifted, preferred_element_type=jnp....  170 us
    all_to_all x1, blocking collectives, stacked_exchange(): arrived = lax.all_to_all(jnp.stack(pieces), axis, 0, 0)  50.3 us
    all_to_all x1, waiting for transfers between devices, on_device(): lax.all_to_all(padded, 'lon', split_axis=0, concat_axis=2, tiled=True)  13.7 us
    dynamic_slice x17, local copies, waits for them, and re-layouts, add_tap(): shifted = lax.dynamic_slice_in_dim(wide, 2 * reach_q - tap, out_cols, 2)  13.6 us
  transfers between devices with their start and end apart: 4, of which 2 were waited for; matrix products, arithmetic and copies ran while one was open for 4% of the time, Pallas kernels for 0%

profile of v1, /device:TPU:2, one launch (start us, length us, event | category | flops | bytes accessed | tf_op | source)
XLA Modules:
  0.0 586.6 jit_solution(397653686185711014)
XLA Ops:
  19.3 7.6 %all-to-all-start = ((bf16[384,18,128]{2,1,0:T(8,128)(2,1)}), bf16[384,18,128]{2,1,0:T(8,128)(2,1)S(1)}, u32[]{:S(2)}, u32[]{:S(2)}) async-start(bf16[384,18,128]{2,1,0:T(8,128)(2,1)} %pad_maximum_fusion), calls=%async_computation | async-start | bytes 4718592 | tf_op jit(solution)/shard_map/all_to_all | solution.py:57
  40.9 13.7 %all-to-all-done = bf16[384,18,128]{2,1,0:T(8,128)(2,1)S(1)} async-done(((bf16[384,18,128]{2,1,0:T(8,128)(2,1)}), bf16[384,18,128]{2,1,0:T(8,128)(2,1)S(1)}, u32[]{:S(2)}, u32[]{:S(2)}) %all-to-all-start) | async-done | bytes 1769504 | tf_op jit(solution)/shard_map/all_to_all | solution.py:57
  65.4 4.8 broadcast_in_dim.17
  70.2 183.4 %while.12 = (s32[]{:T(128)}, f32[3,48,12,1024]{3,2,0,1:T(8,128)}, s32[]{:T(128)}, bf16[48,18,1040]{2,0,1:T(8,128)(2,1)S(1)}, bf16[3,17,12,18]{3,2,0,1:T(8,128)(2...) while((s32[]{:T(128)}, f32[3,48,12,1024]{3,2,0,1:T(8,128)}, s32[]{:T(128)}, ...), condition=%wide.region_2.4_spmd, body=%wide.region_1.3_spmd.sunk | while | flops 65470472 | bytes 21835972 | solution.py:70
  71.0 10.0 %bitcast_add_fusion.2 = f32[3,48,12,1024]{3,2,0,1:T(8,128)} fusion(f32[3,48,12,1024]{3,2,0,1:T(8,128)} %get-tuple-element.160, bf16[48,18,1024]{2,0,1:T(8,128)(2,1)S(1)} %constant_dynamic-slice_fusion.2, bf16[3,17,12,18]{3,2,0,1:T(8,128)(2,1)} %get-tuple-element.173, s32[]{:T(128)S(6)} %select_n.77), kind=kOutput, calls=%fused_computation.3.clone.1 | convolution fusion | flops 65470464 | bytes 18296836 | tf_op jit(solution)/shard_map/while/body/kio,col->kcil/dot_general | solution.py:65
  81.8 10.0 %bitcast_add_fusion.2 = f32[3,48,12,1024]{3,2,0,1:T(8,128)} fusion(f32[3,48,12,1024]{3,2,0,1:T(8,128)} %get-tuple-element.160, bf16[48,18,1024]{2,0,1:T(8,128)(2,1)S(1)} %constant_dynamic-slice_fusion.2, bf16[3,17,12,18]{3,2,0,1:T(8,128)(2,1)} %get-tuple-element.173, s32[]{:T(128)S(6)} %select_n.77), kind=kOutput, calls=%fused_computation.3.clone.1 | convolution fusion | flops 65470464 | bytes 18296836 | tf_op jit(solution)/shard_map/while/body/kio,col->kcil/dot_general | solution.py:65
  92.6 10.0 %bitcast_add_fusion.2 = f32[3,48,12,1024]{3,2,0,1:T(8,128)} fusion(f32[3,48,12,1024]{3,2,0,1:T(8,128)} %get-tuple-element.160, bf16[48,18,1024]{2,0,1:T(8,128)(2,1)S(1)} %constant_dynamic-slice_fusion.2, bf16[3,17,12,18]{3,2,0,1:T(8,128)(2,1)} %get-tuple-element.173, s32[]{:T(128)S(6)} %select_n.77), kind=kOutput, calls=%fused_computation.3.clone.1 | convolution fusion | flops 65470464 | bytes 18296836 | tf_op jit(solution)/shard_map/while/body/kio,col->kcil/dot_general | solution.py:65
  103.4 10.0 %bitcast_add_fusion.2 = f32[3,48,12,1024]{3,2,0,1:T(8,128)} fusion(f32[3,48,12,1024]{3,2,0,1:T(8,128)} %get-tuple-element.160, bf16[48,18,1024]{2,0,1:T(8,128)(2,1)S(1)} %constant_dynamic-slice_fusion.2, bf16[3,17,12,18]{3,2,0,1:T(8,128)(2,1)} %get-tuple-element.173, s32[]{:T(128)S(6)} %select_n.77), kind=kOutput, calls=%fused_computation.3.clone.1 | convolution fusion | flops 65470464 | bytes 18296836 | tf_op jit(solution)/shard_map/while/body/kio,col->kcil/dot_general | solution.py:65
  114.2 10.0 %bitcast_add_fusion.2 = f32[3,48,12,1024]{3,2,0,1:T(8,128)} fusion(f32[3,48,12,1024]{3,2,0,1:T(8,128)} %get-tuple-element.160, bf16[48,18,1024]{2,0,1:T(8,128)(2,1)S(1)} %constant_dynamic-slice_fusion.2, bf16[3,17,12,18]{3,2,0,1:T(8,128)(2,1)} %get-tuple-element.173, s32[]{:T(128)S(6)} %select_n.77), kind=kOutput, calls=%fused_computation.3.clone.1 | convolution fusion | flops 65470464 | bytes 18296836 | tf_op jit(solution)/shard_map/while/body/kio,col->kcil/dot_general | solution.py:65
  125.0 10.0 %bitcast_add_fusion.2 = f32[3,48,12,1024]{3,2,0,1:T(8,128)} fusion(f32[3,48,12,1024]{3,2,0,1:T(8,128)} %get-tuple-element.160, bf16[48,18,1024]{2,0,1:T(8,128)(2,1)S(1)} %constant_dynamic-slice_fusion.2, bf16[3,17,12,18]{3,2,0,1:T(8,128)(2,1)} %get-tuple-element.173, s32[]{:T(128)S(6)} %select_n.77), kind=kOutput, calls=%fused_computation.3.clone.1 | convolution fusion | flops 65470464 | bytes 18296836 | tf_op jit(solution)/shard_map/while/body/kio,col->kcil/dot_general | solution.py:65
  135.7 10.0 %bitcast_add_fusion.2 = f32[3,48,12,1024]{3,2,0,1:T(8,128)} fusion(f32[3,48,12,1024]{3,2,0,1:T(8,128)} %get-tuple-element.160, bf16[48,18,1024]{2,0,1:T(8,128)(2,1)S(1)} %constant_dynamic-slice_fusion.2, bf16[3,17,12,18]{3,2,0,1:T(8,128)(2,1)} %get-tuple-element.173, s32[]{:T(128)S(6)} %select_n.77), kind=kOutput, calls=%fused_computation.3.clone.1 | convolution fusion | flops 65470464 | bytes 18296836 | tf_op jit(solution)/shard_map/while/body/kio,col->kcil/dot_general | solution.py:65
  146.5 10.0 %bitcast_add_fusion.2 = f32[3,48,12,1024]{3,2,0,1:T(8,128)} fusion(f32[3,48,12,1024]{3,2,0,1:T(8,128)} %get-tuple-element.160, bf16[48,18,1024]{2,0,1:T(8,128)(2,1)S(1)} %constant_dynamic-slice_fusion.2, bf16[3,17,12,18]{3,2,0,1:T(8,128)(2,1)} %get-tuple-element.173, s32[]{:T(128)S(6)} %select_n.77), kind=kOutput, calls=%fused_computation.3.clone.1 | convolution fusion | flops 65470464 | bytes 18296836 | tf_op jit(solution)/shard_map/while/body/kio,col->kcil/dot_general | solution.py:65
  157.3 10.0 %bitcast_add_fusion.2 = f32[3,48,12,1024]{3,2,0,1:T(8,128)} fusion(f32[3,48,12,1024]{3,2,0,1:T(8,128)} %get-tuple-element.160, bf16[48,18,1024]{2,0,1:T(8,128)(2,1)S(1)} %constant_dynamic-slice_fusion.2, bf16[3,17,12,18]{3,2,0,1:T(8,128)(2,1)} %get-tuple-element.173, s32[]{:T(128)S(6)} %select_n.77), kind=kOutput, calls=%fused_computation.3.clone.1 | convolution fusion | flops 65470464 | bytes 18296836 | tf_op jit(solution)/shard_map/while/body/kio,col->kcil/dot_general | solution.py:65
  168.1 10.0 %bitcast_add_fusion.2 = f32[3,48,12,1024]{3,2,0,1:T(8,128)} fusion(f32[3,48,12,1024]{3,2,0,1:T(8,128)} %get-tuple-element.160, bf16[48,18,1024]{2,0,1:T(8,128)(2,1)S(1)} %constant_dynamic-slice_fusion.2, bf16[3,17,12,18]{3,2,0,1:T(8,128)(2,1)} %get-tuple-element.173, s32[]{:T(128)S(6)} %select_n.77), kind=kOutput, calls=%fused_computation.3.clone.1 | convolution fusion | flops 65470464 | bytes 18296836 | tf_op jit(solution)/shard_map/while/body/kio,col->kcil/dot_general | solution.py:65
  178.9 10.0 %bitcast_add_fusion.2 = f32[3,48,12,1024]{3,2,0,1:T(8,128)} fusion(f32[3,48,12,1024]{3,2,0,1:T(8,128)} %get-tuple-element.160, bf16[48,18,1024]{2,0,1:T(8,128)(2,1)S(1)} %constant_dynamic-slice_fusion.2, bf16[3,17,12,18]{3,2,0,1:T(8,128)(2,1)} %get-tuple-element.173, s32[]{:T(128)S(6)} %select_n.77), kind=kOutput, calls=%fused_computation.3.clone.1 | convolution fusion | flops 65470464 | bytes 18296836 | tf_op jit(solution)/shard_map/while/body/kio,col->kcil/dot_general | solution.py:65
  189.7 10.0 %bitcast_add_fusion.2 = f32[3,48,12,1024]{3,2,0,1:T(8,128)} fusion(f32[3,48,12,1024]{3,2,0,1:T(8,128)} %get-tuple-element.160, bf16[48,18,1024]{2,0,1:T(8,128)(2,1)S(1)} %constant_dynamic-slice_fusion.2, bf16[3,17,12,18]{3,2,0,1:T(8,128)(2,1)} %get-tuple-element.173, s32[]{:T(128)S(6)} %select_n.77), kind=kOutput, calls=%fused_computation.3.clone.1 | convolution fusion | flops 65470464 | bytes 18296836 | tf_op jit(solution)/shard_map/while/body/kio,col->kcil/dot_general | solution.py:65
  200.5 10.0 %bitcast_add_fusion.2 = f32[3,48,12,1024]{3,2,0,1:T(8,128)} fusion(f32[3,48,12,1024]{3,2,0,1:T(8,128)} %get-tuple-element.160, bf16[48,18,1024]{2,0,1:T(8,128)(2,1)S(1)} %constant_dynamic-slice_fusion.2, bf16[3,17,12,18]{3,2,0,1:T(8,128)(2,1)} %get-tuple-element.173, s32[]{:T(128)S(6)} %select_n.77), kind=kOutput, calls=%fused_computation.3.clone.1 | convolution fusion | flops 65470464 | bytes 18296836 | tf_op jit(solution)/shard_map/while/body/kio,col->kcil/dot_general | solution.py:65
  211.3 10.0 %bitcast_add_fusion.2 = f32[3,48,12,1024]{3,2,0,1:T(8,128)} fusion(f32[3,48,12,1024]{3,2,0,1:T(8,128)} %get-tuple-element.160, bf16[48,18,1024]{2,0,1:T(8,128)(2,1)S(1)} %constant_dynamic-slice_fusion.2, bf16[3,17,12,18]{3,2,0,1:T(8,128)(2,1)} %get-tuple-element.173, s32[]{:T(128)S(6)} %select_n.77), kind=kOutput, calls=%fused_computation.3.clone.1 | convolution fusion | flops 65470464 | bytes 18296836 | tf_op jit(solution)/shard_map/while/body/kio,col->kcil/dot_general | solution.py:65
  222.1 10.0 %bitcast_add_fusion.2 = f32[3,48,12,1024]{3,2,0,1:T(8,128)} fusion(f32[3,48,12,1024]{3,2,0,1:T(8,128)} %get-tuple-element.160, bf16[48,18,1024]{2,0,1:T(8,128)(2,1)S(1)} %constant_dynamic-slice_fusion.2, bf16[3,17,12,18]{3,2,0,1:T(8,128)(2,1)} %get-tuple-element.173, s32[]{:T(128)S(6)} %select_n.77), kind=kOutput, calls=%fused_computation.3.clone.1 | convolution fusion | flops 65470464 | bytes 18296836 | tf_op jit(solution)/shard_map/while/body/kio,col->kcil/dot_general | solution.py:65
  232.9 10.0 %bitcast_add_fusion.2 = f32[3,48,12,1024]{3,2,0,1:T(8,128)} fusion(f32[3,48,12,1024]{3,2,0,1:T(8,128)} %get-tuple-element.160, bf16[48,18,1024]{2,0,1:T(8,128)(2,1)S(1)} %constant_dynamic-slice_fusion.2, bf16[3,17,12,18]{3,2,0,1:T(8,128)(2,1)} %get-tuple-element.173, s32[]{:T(128)S(6)} %select_n.77), kind=kOutput, calls=%fused_computation.3.clone.1 | convolution fusion | flops 65470464 | bytes 18296836 | tf_op jit(solution)/shard_map/while/body/kio,col->kcil/dot_general | solution.py:65
  243.6 10.0 %bitcast_add_fusion.2 = f32[3,48,12,1024]{3,2,0,1:T(8,128)} fusion(f32[3,48,12,1024]{3,2,0,1:T(8,128)} %get-tuple-element.160, bf16[48,18,1024]{2,0,1:T(8,128)(2,1)S(1)} %constant_dynamic-slice_fusion.2, bf16[3,17,12,18]{3,2,0,1:T(8,128)(2,1)} %get-tuple-element.173, s32[]{:T(128)S(6)} %select_n.77), kind=kOutput, calls=%fused_computation.3.clone.1 | convolution fusion | flops 65470464 | bytes 18296836 | tf_op jit(solution)/shard_map/while/body/kio,col->kcil/dot_general | solution.py:65
  253.6 7.4 %copy.60 = bf16[3,48,12,1024]{3,1,2,0:T(8,128)(2,1)S(1)} copy(f32[3,48,12,1024]{3,2,0,1:T(8,128)} %get-tuple-element.71) | data formatting | bytes 10616832 | tf_op jit(solution)/shard_map/while | solution.py:70
  262.3 50.3 %all_to_all.23 = bf16[8,3,48,12,128]{4,2,3,1,0:T(8,128)(2,1)S(1)} all-to-all(bf16[8,3,48,12,128]{4,2,3,1,0:T(8,128)(2,1)S(1)} %fusion.7), channel_id=1, replica_groups=mesh['lat'=32,'lon'=8] {'lon'}, dimensions={0} | all-to-all | bytes 7077888 | tf_op jit(solution)/shard_map/all_to_all | solution.py:9
  324.2 252.7 %all-reduce.2.cloned.1.call-done = f32[3,384,384]{2,1,0:T(8,128)} async-done(((f32[3,384,384]{2,1,0:T(8,128)}), f32[3,384,384]{2,1,0:T(8,128)}) %all-reduce.2.cloned.1.call-update) | async-done | bytes 1769488 | tf_op jit(solution)/shard_map/psum | solution.py:81
  (72 shorter events, 64.7 us)
Async XLA Ops:
  7.2 308.2 %copy-start = (bf16[384,12,128]{2,0,1:T(8,128)(2,1)S(1)}, bf16[384,12,128]{2,0,1:T(8,128)(2,1)}, u32[]{:S(2)}) copy-start(bf16[384,12,128]{2,0,1:T(8,128)(2,1)} %param.11) | copy-start | bytes 3538948
  9.1 5.8 collective-permute-start
  11.5 4.6 collective-permute-start.1
  19.3 7.6 %copy-start.1 = (s32[384]{0:T(512)S(1)}, s32[384]{0:T(512)}, u32[]{:S(2)}) copy-start(s32[384]{0:T(512)} %param.14) | copy-start | bytes 4612
  19.3 8.3 %copy-start.2 = (s32[384]{0:T(512)S(1)}, s32[384]{0:T(512)}, u32[]{:S(2)}) copy-start(s32[384]{0:T(512)} %param.15) | copy-start | bytes 4612
  19.3 35.4 %all-to-all-start = ((bf16[384,18,128]{2,1,0:T(8,128)(2,1)}), bf16[384,18,128]{2,1,0:T(8,128)(2,1)S(1)}, u32[]{:S(2)}, u32[]{:S(2)}) async-start(bf16[384,18,128]{2,1,0:T(8,128)(2,1)} %pad_maximum_fusion), calls=%async_computation | async-start | bytes 4718592 | tf_op jit(solution)/shard_map/all_to_all | solution.py:57
  26.9 550.0 %all-reduce.2.cloned.1.call-start = ((), (), s32[]{:S(2)}) async-start(), calls=%async_computation.2 | async-start | bytes 3538944 | tf_op jit(solution)/shard_map/psum | solution.py:81
  59.7 1.3 copy-start.4
  313.6 1.7 copy-start.3
  315.3 3.3 copy-start.5
Sparse Core Ops, SparseCore 0:
  318.7 258.1 all-reduce.1
